TPU v7x, 128 devices: a whole 4x4x4 slice. The times are simulated.
128 devices in a mesh: dp: 8 (over x, y_lo), pp: 8 (over y_hi, z), tp: 2 (over core).
Axes of the slice: x: 4, y: 4 (y_hi: 2, y_lo: 2; y = y_hi * 2 + y_lo), z: 4, core: 2. Of those that a mesh axis runs over, the one named last changes fastest.
Arguments:
- hidden_in: bfloat16 [8, 4096, 8192], P('pp', 'dp'), may hold values from -6 to 6
- queries: bfloat16 [8, 4096, 4096], P('pp', 'dp', 'tp'), may hold values from -300 to 300
- out_grad: bfloat16 [8, 4096, 4096], P('pp', 'dp', 'tp'), may hold values from -6 to 6
- key_weight: bfloat16 [8, 8192, 512], P('pp', 'dp', 'tp'), may hold values from -0.0625 to 0.0625
- value_weight: bfloat16 [8, 8192, 512], P('pp', 'dp', 'tp'), may hold values from -0.0625 to 0.0625
- doc_lengths: int32 [8, 8, 8], P('pp', 'dp'), may hold values from 1 to 96, 512 in all within a row
Outputs:
- query_grad: bfloat16 [8, 4096, 4096], P('pp', 'dp', 'tp')
- input_grad: bfloat16 [8, 4096, 8192], P('pp', 'dp', 'tp')
- key_weight_grad: float32 [8, 8192, 512], P('pp', 'dp', 'tp')
- value_weight_grad: float32 [8, 8192, 512], P('pp', 'dp', 'tp')
Inputs may be any that keep to these rules, and one draw needn't show every extreme that they name: `doc_lengths`: in every section and relay the 8 lengths fill the 512 rows; in every sequence some document has exactly 96 rows.
All inputs are finite; a program needn't handle non-finite values.
Results may differ from a plain program's by a relative error of at most 0.034.
The roundings to bfloat16 on the way count: a program that leaves them out, or rounds other values in their place, can miss the bound.
Values may be sent and summed in bfloat16 or wider, within the bound.
A program may use at most 128 MiB of HBM per device.

v0:
```python
import jax
import jax.numpy as jnp
from jax import lax
from jax.sharding import PartitionSpec as P

HD = 128


def shifted(block, axis, distance):
    devices = range(lax.axis_size(axis))
    route = [((i - distance) % len(devices), i) for i in devices]
    return lax.ppermute(block, axis, route)


def attend(query_in, grad_in, key_in, value_in, allowed):
    slot_count, row_count, kv_heads, query_width = query_in.shape
    head_dim = key_in.shape[3]
    group_size = query_width // head_dim
    score_scale = head_dim ** (-0.5)
    query_five = query_in.reshape(slot_count, row_count, kv_heads, group_size, head_dim)
    grad_five = grad_in.reshape(slot_count, row_count, kv_heads, group_size, head_dim)
    scores = (
        jnp.einsum("bqkge,bpke->bkgqp", query_five, key_in, preferred_element_type=jnp.float32)
        * score_scale
    )
    scores = jnp.where(allowed[:, None, None], scores, -1e30)
    row_top = jnp.max(scores, axis=-1, keepdims=True)
    raised = jnp.exp(scores - row_top)
    attn_probs = raised / jnp.sum(raised, axis=-1, keepdims=True)
    probs_low = attn_probs.astype(jnp.bfloat16)
    attn_out = jnp.einsum(
        "bkgqp,bpke->bqkge", probs_low, value_in, preferred_element_type=jnp.float32
    )
    row_delta = jnp.transpose(
        jnp.sum(grad_five.astype(jnp.float32) * attn_out, axis=-1), (0, 2, 3, 1)
    )
    dprobs = jnp.einsum(
        "bqkge,bpke->bkgqp", grad_five, value_in, preferred_element_type=jnp.float32
    )
    dscores = (attn_probs * (dprobs - row_delta[..., None])).astype(jnp.bfloat16)
    grad_query = (
        jnp.einsum("bkgqp,bpke->bqkge", dscores, key_in, preferred_element_type=jnp.float32)
        * score_scale
    )
    grad_query = grad_query.astype(jnp.bfloat16).reshape(
        slot_count, row_count, kv_heads, query_width
    )
    grad_key = (
        jnp.einsum("bkgqp,bqkge->bpke", dscores, query_five, preferred_element_type=jnp.float32)
        * score_scale
    ).astype(jnp.bfloat16)
    grad_value = jnp.einsum(
        "bkgqp,bqkge->bpke", probs_low, grad_five, preferred_element_type=jnp.float32
    ).astype(jnp.bfloat16)
    return (grad_query, grad_key, grad_value)


def body(hidden_in, queries, out_grad, key_weight, value_weight, doc_lengths):
    hidden = hidden_in[0]
    query_rows = queries[0]
    grad_rows = out_grad[0]
    lengths = doc_lengths[0, 0]
    seq_rows = hidden.shape[0]
    kv_width = key_weight.shape[2]
    kv_local = kv_width // HD
    pipe_count = lax.axis_size("dp")
    stacked = jnp.concatenate((key_weight[0], value_weight[0]), axis=1)
    hidden_cols = hidden
    projected = jnp.dot(
        hidden_cols,
        lax.all_gather(stacked, "dp", axis=0, tiled=True),
        preferred_element_type=jnp.float32,
    )
    projected = projected.astype(jnp.bfloat16)
    key_rows = projected[:, :kv_width]
    value_rows = projected[:, kv_width:]
    doc_ends = jnp.cumsum(lengths)
    positions = jnp.arange(seq_rows, dtype=jnp.int32)
    segment = jnp.sum((positions[:, None] >= doc_ends[None, :]).astype(jnp.int32), axis=1)
    allowed = ((segment[:, None] == segment[None, :]) & (positions[None, :] <= positions[:, None]))[
        None
    ]
    query_four = query_rows.reshape(1, seq_rows, kv_local, -1)
    grad_four = grad_rows.reshape(1, seq_rows, kv_local, -1)
    key_four = key_rows.reshape(1, seq_rows, kv_local, HD)
    value_four = value_rows.reshape(1, seq_rows, kv_local, HD)
    query_parts = []
    key_parts = []
    value_parts = []
    for kv_head in range(kv_local):
        outcome = attend(
            query_four[:, :, kv_head : kv_head + 1],
            grad_four[:, :, kv_head : kv_head + 1],
            key_four[:, :, kv_head : kv_head + 1],
            value_four[:, :, kv_head : kv_head + 1],
            allowed,
        )
        query_parts.append(outcome[0])
        key_parts.append(outcome[1])
        value_parts.append(outcome[2])
    grad_query = jnp.concatenate(query_parts, axis=2).reshape(seq_rows, -1)
    grad_key = jnp.concatenate(key_parts, axis=2).reshape(seq_rows, -1)
    grad_value = jnp.concatenate(value_parts, axis=2).reshape(seq_rows, -1)
    joined_grad = jnp.concatenate((grad_key, grad_value), axis=1)
    partial_in = lax.dot_general(
        joined_grad,
        lax.all_gather(stacked, "dp", axis=0, tiled=True),
        (((1,), (1,)), ((), ())),
        preferred_element_type=jnp.float32,
    )
    summed = lax.psum_scatter(
        partial_in.astype(jnp.bfloat16), "tp", scatter_dimension=1, tiled=True
    )
    earlier = shifted(summed, "pp", -1)
    grad_scale = (seq_rows * pipe_count) ** (-0.5)
    hidden_cols = hidden
    product = lax.dot_general(
        hidden_cols, joined_grad, (((0,), (0,)), ((), ())), preferred_element_type=jnp.float32
    )
    weight_grads = lax.psum_scatter(
        (product * grad_scale).astype(jnp.bfloat16), "dp", scatter_dimension=0, tiled=True
    ).astype(jnp.float32)
    return (
        grad_query[None],
        earlier[None],
        weight_grads[:, :kv_width][None],
        weight_grads[:, kv_width:][None],
    )


def solution(mesh):
    return jax.shard_map(
        body,
        mesh=mesh,
        in_specs=(
            P("pp", "dp", None),
            P("pp", "dp", "tp"),
            P("pp", "dp", "tp"),
            P("pp", "dp", "tp"),
            P("pp", "dp", "tp"),
            P("pp", "dp", None),
        ),
        out_specs=(
            P("pp", "dp", "tp"),
            P("pp", "dp", "tp"),
            P("pp", "dp", "tp"),
            P("pp", "dp", "tp"),
        ),
        check_vma=False,
    )
```

profile of v0, /device:TPU:1, one launch (start us, length us, event | category | flops | bytes accessed | tf_op | source)
XLA Modules:
  0.0 524.6 jit_solution(17410473411778906031)
XLA Ops:
  7.2 2.2 pad_maximum_fusion.1
  9.5 3.9 copy.61
  13.5 2.9 copy.64
  16.8 2.7 fusion.72
  19.6 1.4 fusion.71
  21.0 160.8 %all-gather.2.cloned.1.call-done = bf16[8192,512]{1,0:T(8,128)(2,1)} async-done(((bf16[1024,512]{1,0:T(8,128)(2,1)}), bf16[8192,512]{1,0:T(8,128)(2,1)}) %all-gather.2.cloned.1.call-update) | async-done | bytes 8388624 | tf_op jit(solution)/shard_map/all_gather | solution.py:71
  181.8 10.3 %fusion.35 = bf16[512,512]{0,1:T(8,128)(2,1)S(1)} fusion(bf16[8192,512]{1,0:T(8,128)(2,1)} %all-gather.2.cloned.1.call-done, bf16[1,512,8192]{2,1,0:T(8,128)(2,1)} %param.6), kind=kOutput, calls=%fused_computation.42 | convolution fusion | flops 4295229440 | bytes 17301504 | tf_op jit(solution)/shard_map/dot_general | solution.py:69
  192.2 1.6 fusion.12
  193.8 3.7 fusion.9
  197.5 1.9 fusion.11
  199.4 2.6 fusion.57
  202.0 2.8 fusion.26
  204.8 3.1 fusion.15
  208.0 1.4 fusion.61
  209.4 2.8 fusion.27
  212.3 2.6 fusion.54
  214.9 3.1 fusion.14
  218.0 2.0 copy-done.1
  220.0 1.5 fusion.60
  221.5 10.2 %convolution_convert_fusion = bf16[512,8192]{1,0:T(8,128)(2,1)} fusion(bf16[8192,512]{1,0:T(8,128)(2,1)} %all-gather.2.cloned.1.call-done, bf16[512,256]{0,1:T(8,128)(2,1)S(1)} %bitcast.288, bf16[512,256]{0,1:T(8,128)(2,1)S(1)} %bitcast.286), kind=kOutput, calls=%fused_computation.1 | convolution fusion | flops 4300210176 | bytes 17301504 | tf_op jit(solution)/shard_map/dot_general | solution.py:105
  231.8 10.7 %fusion = bf16[8192,512]{0,1:T(8,128)(2,1)} fusion(bf16[1,512,8192]{2,1,0:T(8,128)(2,1)} %param.6, bf16[512,256]{0,1:T(8,128)(2,1)S(1)} %bitcast.289, bf16[512,256]{0,1:T(8,128)(2,1)S(1)} %bitcast.287), kind=kOutput, calls=%fused_computation.2 | convolution fusion | flops 4304404480 | bytes 17301504 | tf_op jit(solution)/shard_map/dot_general | solution.py:117
  242.5 14.7 %reduce-scatter.3.cloned.1.call-done = bf16[512,4096]{1,0:T(8,128)(2,1)} async-done(((bf16[512,8192]{1,0:T(8,128)(2,1)}), bf16[512,4096]{1,0:T(8,128)(2,1)}) %reduce-scatter.3.cloned.1.call-update) | async-done | bytes 4194320 | tf_op jit(solution)/shard_map/reduce_scatter | solution.py:111
  257.2 5.2 collective-permute-start
  262.4 2.9 multiply_convert_fusion.1
  265.4 2.9 multiply_convert_fusion.2
  268.5 2.4 copy.105
  270.8 238.1 %reduce-scatter.5.cloned.1.call-done = bf16[1024,512]{0,1:T(8,128)(2,1)} async-done(((bf16[8192,512]{0,1:T(8,128)(2,1)}), bf16[1024,512]{0,1:T(8,128)(2,1)}) %reduce-scatter.5.cloned.1.call-update) | async-done | bytes 1048592 | tf_op jit(solution)/shard_map/reduce_scatter | solution.py:120
  509.0 1.5 convert_element_type.163
  510.5 0.2 slice_bitcast_fusion
  510.7 1.3 copy.84
  512.0 1.3 copy.83
  513.3 4.7 copy.111
  (25 shorter events, 1.0 us)
Async XLA Ops:
  7.2 9.2 %copy-start.5 = (s32[1,1,8]{2,1,0:T(1,128)S(1)}, s32[1,1,8]{2,1,0:T(1,128)}, u32[]{:S(2)}) copy-start(s32[1,1,8]{2,1,0:T(1,128)} %param.11) | copy-start | bytes 100
  7.2 174.6 %all-gather.2.cloned.1.call-start = ((), (), s32[]{:S(2)}) async-start(), calls=%async_computation.2 | async-start | bytes 9437184 | tf_op jit(solution)/shard_map/all_gather | solution.py:71
  9.5 247.7 %reduce-scatter.3.cloned.1.call-start = ((), (), s32[]{:S(2)}) async-start(), calls=%async_computation.3 | async-start | bytes 12582912 | tf_op jit(solution)/shard_map/reduce_scatter | solution.py:111
  192.1 1.6 copy-start.3
  197.4 2.0 copy-start.4
  204.8 4.6 copy-start.2
  207.9 4.3 copy-start
  218.0 2.0 copy-start.1
  231.7 277.3 %reduce-scatter.5.cloned.1.call-start = ((), (), s32[]{:S(2)}) async-start(), calls=%async_computation.4 | async-start | bytes 9437184 | tf_op jit(solution)/shard_map/reduce_scatter | solution.py:120
  257.2 256.1 %collective-permute-start = (bf16[512,4096]{1,0:T(8,128)(2,1)}, bf16[512,4096]{1,0:T(8,128)(2,1)}, u32[]{:S(2)}, u32[]{:S(2)}) collective-permute-start(bf16[512,4096]{1,0:T(8,128)(2,1)} %reduce-scatter.3.cloned.1.call-done), channel_id=1, source_target_pairs={{2,0},{4,2},{6,4},{8,6},{10,8},{12,10},{14,12},{0,14},{3,1},{5,3},... | collective-permute-start | bytes 12582920 | tf_op jit(solution)/shard_map/ppermute | solution.py:12
Sparse Core Ops, SparseCore 0:
  10.2 171.5 all-gather.1
  231.9 25.2 reduce-scatter.2
  259.7 249.2 reduce-scatter.4
where the time goes:
time: 525 us
  waiting for transfers between devices  414 us (79%)
  matrix products  62.2 us (12%)
  local copies, waits for them, and re-layouts  22.9 us (4%)
  between operations  14 us (3%)
  other arithmetic  6.37 us (1%)
  starting transfers between devices  5.36 us (1%)
    reduce_scatter x1, waiting for transfers between devices, body(): lax.psum_scatter((product * grad_scale).astype(jnp.bfloat16), 'dp', scatt...  238 us
    all_gather x1, waiting for transfers between devices, body(): lax.all_gather(stacked, 'dp', axis=0, tiled=True)  161 us
    unnamed x17, local copies, waits for them, and re-layouts  16.1 us
    reduce_scatter x1, waiting for transfers between devices, body(): lax.psum_scatter(partial_in.astype(jnp.bfloat16), 'tp', scatter_dimension...  14.7 us
    dot_general x1, matrix products, body(): lax.dot_general(hidden_cols, joined_grad, (((0,), (0,)), ((), ())), prefe...  10.7 us
  transfers between devices with their start and end apart: 4, of which 3 were waited for; matrix products, arithmetic and copies ran while one was open for 7% of the time, Pallas kernels for 0%

commit v1 on v0

v1 whole, which is shorter than its diff:
```python
import functools

import jax
import jax.numpy as jnp
from jax import lax
from jax.experimental import pallas as pl
from jax.experimental.pallas import tpu as pltpu
from jax.sharding import PartitionSpec as P

HD = 128
ROWS = 512
WIDTH = 8192
SHARD = 1024
HALF = 512
GROUP = 8
TILE = 512
TILES = 8
MESH = pl.DeviceIdType.MESH
NT = (((1,), (1,)), ((), ()))
TN = (((0,), (0,)), ((), ()))

GATHER = ("p0a", "p0b", "m0a", "m0b", "y0a", "y0b", "p1a", "m1b", "p2a", "p2b", "m2a", "m2b", "y2a", "y2b")
SCATTER = ("y1", "p1", "m1", "p2", "m2", "y3", "p3k", "p3v", "m3k", "m3v")
PER_HEAD = len(GATHER) + len(SCATTER)
TP_SEM = 2 * PER_HEAD
PP_SEM = TP_SEM + TILES
REMOTE_SEMS = PP_SEM + TILES
HID_SEM, Q_SEM, G_SEM, W_SEM, DQ_SEM, WG_SEM = 0, 8, 9, 10, 14, 16
LOCAL_SEMS = 18


def kernel(
    hidden_ref, query_ref, grad_ref, kw_ref, vw_ref, len_ref,
    dq_ref, lg_ref, wk_ref, wv_ref,
    hid, qs, gs, dqs, wg, kv, acc, bias, gacc, gkv, gkvt, prod,
    ry1, rp1, rm1, rp2, rm2, ry3, rp3, rm3,
    lgs, lgr, lgo, wks, wvs, ssem, rsem, lsem,
):
    dp, pp, tp = lax.axis_index("dp"), lax.axis_index("pp"), lax.axis_index("tp")
    x, y = dp // 2, dp % 2
    xp, xm, x2, yq = (x + 1) % 4, (x + 3) % 4, (x + 2) % 4, 1 - y
    j_me, j_p, j_m, j_2 = dp, xp * 2 + y, xm * 2 + y, x2 * 2 + y
    j_q, j_pq, j_mq, j_2q = x * 2 + yq, xp * 2 + yq, xm * 2 + yq, x2 * 2 + yq
    dev_p, dev_m, dev_y = (j_p, pp, tp), (j_m, pp, tp), (j_q, pp, tp)
    dev_t = (dp, pp, 1 - tp)
    dev_prev, dev_next = (dp, (pp + 7) % 8, tp), (dp, (pp + 1) % 8, tp)

    sent = []

    def remote(src, dst, k, dev):
        return pltpu.make_async_remote_copy(
            src_ref=src, dst_ref=dst, send_sem=ssem.at[k], recv_sem=rsem.at[k],
            device_id=dev, device_id_type=MESH,
        )

    def local(src, dst, k):
        return pltpu.make_async_copy(src, dst, lsem.at[k])

    w_copies = []
    for h in range(2):
        for n, ref in enumerate((kw_ref, vw_ref)):
            c = local(ref.at[:, pl.ds(h * HD, HD)], wg.at[h, j_me, :, pl.ds(n * HD, HD)], W_SEM + 2 * h + n)
            c.start()
            w_copies.append(c)
    hid_copies = []
    for j in range(8):
        c = local(hidden_ref.at[:, pl.ds(j * SHARD, SHARD)], hid.at[:, pl.ds(j * SHARD, SHARD)], HID_SEM + j)
        c.start()
        hid_copies.append(c)
    q_copy = local(query_ref, qs, Q_SEM)
    g_copy = local(grad_ref, gs, G_SEM)
    q_copy.start()
    g_copy.start()

    barrier = pltpu.get_barrier_semaphore()
    for dev in (dev_p, dev_m, dev_y, dev_t, dev_prev, dev_next):
        pl.semaphore_signal(barrier, inc=1, device_id=dev, device_id_type=MESH)
    pl.semaphore_wait(barrier, 6)

    def gather_copy(h, name):
        dev = {"p": dev_p, "m": dev_m, "y": dev_y}[name[0]]
        j = {"p0": j_me, "m0": j_me, "y0": j_me, "p1": j_m, "m1": j_p, "p2": j_q, "m2": j_q, "y2": j_2}[name[:2]]
        rows = pl.ds(0 if name[2] == "a" else HALF, HALF)
        block = wg.at[h, j, rows]
        return remote(block, block, h * PER_HEAD + GATHER.index(name), dev)

    def gather_start(h, *names):
        for name in names:
            c = gather_copy(h, name)
            c.start()
            sent.append(c)

    def gather_wait(h, *names):
        for name in names:
            gather_copy(h, name).wait_recv()

    def project(h, j, first=False):
        columns = pl.ds(pl.multiple_of(j * SHARD, SHARD), SHARD)
        term = jnp.dot(hid[:, columns], wg[h, j], preferred_element_type=jnp.float32)
        if first:
            acc[...] = term
        else:
            acc[...] += term

    def attend(h, b):
        w0 = 128 * max(b - 1, 0)
        window = pl.ds(w0, 256)

        def pair(i, carry):
            c0 = pl.multiple_of((h * GROUP + 2 * i) * HD, 2 * HD)
            rows = pl.ds(b * 128, 128)
            q2 = jnp.concatenate([qs[rows, pl.ds(c0, HD)], qs[rows, pl.ds(c0 + HD, HD)]], axis=0)
            g2 = jnp.concatenate([gs[rows, pl.ds(c0, HD)], gs[rows, pl.ds(c0 + HD, HD)]], axis=0)
            keys = kv[h, window, pl.ds(0, HD)]
            values = kv[h, window, pl.ds(HD, HD)]
            mask = bias[b]
            s = lax.dot_general(keys, q2, NT, preferred_element_type=jnp.float32)
            s = s * (HD ** -0.5) + jnp.concatenate([mask, mask], axis=1)
            top = jnp.max(s, axis=0, keepdims=True)
            e = jnp.exp(s - top)
            p = e * (1.0 / jnp.sum(e, axis=0, keepdims=True))
            low = p.astype(jnp.bfloat16)
            dpr = lax.dot_general(values, g2, NT, preferred_element_type=jnp.float32)
            delta = jnp.sum(low.astype(jnp.float32) * dpr, axis=0, keepdims=True)
            ds = (p * (dpr - delta)).astype(jnp.bfloat16)
            dq = lax.dot_general(ds, keys, TN, preferred_element_type=jnp.float32) * (HD ** -0.5)
            dq = dq.astype(jnp.bfloat16)
            dqs[rows, pl.ds(c0, HD)] = dq[:128]
            dqs[rows, pl.ds(c0 + HD, HD)] = dq[128:]
            gacc[window, pl.ds(0, HD)] += jnp.dot(ds, q2, preferred_element_type=jnp.float32)
            gacc[window, pl.ds(HD, HD)] += jnp.dot(low, g2, preferred_element_type=jnp.float32)
            return carry

        lax.fori_loop(0, GROUP // 2, pair, 0)

    def finish_head(h):
        columns = pl.ds(h * GROUP * HD, GROUP * HD)
        local(dqs.at[:, columns], dq_ref.at[:, columns], DQ_SEM + h).start()
        key_part = gacc[:, pl.ds(0, HD)] * (HD ** -0.5)
        value_part = gacc[:, pl.ds(HD, HD)]
        gkv[h, :, pl.ds(0, HD)] = key_part.astype(jnp.bfloat16)
        gkv[h, :, pl.ds(HD, HD)] = value_part.astype(jnp.bfloat16)
        gkvt[h, pl.ds(0, HD), :] = key_part.T.astype(jnp.bfloat16)
        gkvt[h, pl.ds(HD, HD), :] = value_part.T.astype(jnp.bfloat16)

    targets = (j_2q, j_pq, j_mq, j_2, j_q, j_p, j_m)

    def term(h, j):
        columns = pl.ds(pl.multiple_of(j * SHARD, SHARD), SHARD)
        out = jnp.dot(gkvt[h], hid[:, columns], preferred_element_type=jnp.float32)
        return (out * ((ROWS * 8) ** -0.5)).astype(jnp.bfloat16)

    def terms(h, *slots):
        for n in slots:
            prod[h, n] = term(h, targets[n])

    krows, vrows = pl.ds(0, HD), pl.ds(HD, HD)

    def scatter_copy(h, name):
        src, dst, dev = {
            "y1": (prod.at[h, 0], ry1.at[h], dev_y),
            "p1": (prod.at[h, 1], rp1.at[h], dev_p),
            "m1": (prod.at[h, 2], rm1.at[h], dev_m),
            "p2": (prod.at[h, 3, krows], rp2.at[h], dev_p),
            "m2": (prod.at[h, 3, vrows], rm2.at[h], dev_m),
            "y3": (prod.at[h, 4], ry3.at[h], dev_y),
            "p3k": (prod.at[h, 5, krows], rp3.at[h, krows], dev_p),
            "p3v": (prod.at[h, 5, vrows], rp3.at[h, vrows], dev_p),
            "m3k": (prod.at[h, 6, krows], rm3.at[h, krows], dev_m),
            "m3v": (prod.at[h, 6, vrows], rm3.at[h, vrows], dev_m),
        }[name]
        return remote(src, dst, h * PER_HEAD + len(GATHER) + SCATTER.index(name), dev)

    def scatter_start(h, *names):
        for name in names:
            c = scatter_copy(h, name)
            c.start()
            sent.append(c)

    def scatter_wait(h, *names):
        for name in names:
            scatter_copy(h, name).wait_recv()

    def wide(block):
        return block.astype(jnp.float32)

    def scatter_first(h):
        terms(h, 0, 1, 2)
        scatter_start(h, "y1", "p1", "m1")

    def scatter_rest_terms(h):
        terms(h, 3, 4, 5, 6)
        scatter_start(h, "p3v", "m3k")

    def scatter_second(h):
        scatter_wait(h, "y1")
        prod[h, 3] = (wide(prod[h, 3]) + wide(ry1[h])).astype(jnp.bfloat16)
        scatter_start(h, "p2", "m2")
        scatter_wait(h, "p1", "m1")
        prod[h, 4] = (wide(prod[h, 4]) + wide(rp1[h]) + wide(rm1[h])).astype(jnp.bfloat16)
        scatter_start(h, "y3")

    def scatter_third(h):
        scatter_wait(h, "p2", "m2")
        prod[h, 5, krows] = (wide(prod[h, 5, krows]) + wide(rp2[h])).astype(jnp.bfloat16)
        scatter_start(h, "p3k")
        prod[h, 6, vrows] = (wide(prod[h, 6, vrows]) + wide(rm2[h])).astype(jnp.bfloat16)
        scatter_start(h, "m3v")

    def scatter_last(h):
        own = term(h, j_me)
        scatter_wait(h, "y3", "p3k", "p3v", "m3k", "m3v")
        total = wide(own) + wide(ry3[h]) + wide(rp3[h]) + wide(rm3[h])
        wks[:, pl.ds(h * HD, HD)] = total[:HD].T
        wvs[:, pl.ds(h * HD, HD)] = total[HD:].T

    for c in w_copies:
        c.wait()
    gather_start(0, "p0a", "p0b", "m0a", "m0b", "y0a", "y0b")
    ends, last = [], jnp.int32(0)
    for k in range(8):
        last = last + len_ref[0, k]
        ends.append(last)
    for b in range(4):
        w0 = 128 * max(b - 1, 0)
        key_at = lax.broadcasted_iota(jnp.int32, (256, 128), 0) + w0
        query_at = lax.broadcasted_iota(jnp.int32, (256, 128), 1) + b * 128
        key_doc = jnp.zeros((256, 128), jnp.int32)
        query_doc = jnp.zeros((256, 128), jnp.int32)
        for end in ends:
            key_doc += (key_at >= end).astype(jnp.int32)
            query_doc += (query_at >= end).astype(jnp.int32)
        bias[b] = jnp.where((key_doc == query_doc) & (key_at <= query_at), 0.0, -1e30)
    for c in hid_copies:
        c.wait()
    project(0, j_me, True)
    gather_wait(0, "p0a", "m0a")
    gather_start(0, "p1a")
    gather_wait(0, "y0a")
    gather_start(0, "p2a", "m2a")
    gather_wait(0, "m0b")
    gather_start(0, "m1b")
    gather_wait(0, "p0b", "y0b")
    gather_start(0, "p2b", "m2b")
    for j in (j_m, j_p, j_q):
        project(0, j)
    gather_wait(0, "p1a")
    gather_start(0, "y2a")
    gather_wait(0, "m1b")
    gather_start(0, "y2b")
    project(0, j_2)
    gather_wait(0, "p2a", "m2a")
    gather_start(1, "p0a", "p0b", "m0a", "m0b")
    gather_wait(0, "y2a")
    gather_start(1, "y0a", "y0b")
    gather_wait(0, "p2b", "m2b")
    project(0, j_pq)
    project(0, j_mq)
    gather_wait(0, "y2b")
    project(0, j_2q)
    kv[0] = acc[...].astype(jnp.bfloat16)
    q_copy.wait()
    g_copy.wait()

    gacc[...] = jnp.zeros_like(gacc)
    attend(0, 0)
    gather_wait(1, "p0a", "m0a")
    gather_start(1, "p1a")
    gather_wait(1, "y0a")
    gather_start(1, "p2a", "m2a")
    attend(0, 1)
    gather_wait(1, "m0b")
    gather_start(1, "m1b")
    gather_wait(1, "p0b", "y0b")
    gather_start(1, "p2b", "m2b")
    attend(0, 2)
    gather_wait(1, "p1a")
    gather_start(1, "y2a")
    gather_wait(1, "m1b")
    gather_start(1, "y2b")
    attend(0, 3)
    finish_head(0)
    terms(0, 0, 1, 2)
    project(1, j_me, True)
    for j in (j_m, j_p, j_q, j_2):
        project(1, j)
    gather_wait(1, "p2a", "m2a", "y2a")
    scatter_start(0, "y1", "p1", "m1")
    terms(0, 3, 4, 5, 6)
    gather_wait(1, "p2b", "m2b")
    project(1, j_pq)
    project(1, j_mq)
    gather_wait(1, "y2b")
    project(1, j_2q)
    kv[1] = acc[...].astype(jnp.bfloat16)
    scatter_start(0, "p3v", "m3k")

    gacc[...] = jnp.zeros_like(gacc)
    attend(1, 0)
    attend(1, 1)
    scatter_second(0)
    attend(1, 2)
    attend(1, 3)
    finish_head(1)

    def tp_copy(t):
        return remote(lgs.at[t], lgr.at[t], TP_SEM + t, dev_t)

    def pp_copy(t):
        columns = pl.ds(pl.multiple_of(t * TILE, TILE), TILE)
        return remote(lgo.at[t], lg_ref.at[:, columns], PP_SEM + t, dev_prev)

    def layer_tile(half, t):
        j = half * 4 + t // 2
        rows = pl.ds(pl.multiple_of((t % 2) * TILE, TILE), TILE)
        return lax.dot_general(gkv[0], wg[0, j, rows], NT, preferred_element_type=jnp.float32) + lax.dot_general(
            gkv[1], wg[1, j, rows], NT, preferred_element_type=jnp.float32
        )

    def layer_step(t, carry):
        @pl.when(t < TILES)
        def _():
            lgs[t] = layer_tile(1 - tp, t).astype(jnp.bfloat16)
            tp_copy(t).start()
            lgo[t] = layer_tile(tp, t).astype(jnp.bfloat16)

        @pl.when(t > 0)
        def _():
            tp_copy(t - 1).wait_recv()
            lgo[t - 1] = (wide(lgo[t - 1]) + wide(lgr[t - 1])).astype(jnp.bfloat16)
            pp_copy(t - 1).start()

        return carry

    lax.fori_loop(0, TILES + 1, layer_step, 0)

    scatter_third(0)
    terms(1, 0, 1, 2)
    scatter_start(1, "y1", "p1", "m1")
    scatter_last(0)
    scatter_rest_terms(1)
    scatter_second(1)
    scatter_third(1)
    scatter_last(1)
    wk_copy = local(wks, wk_ref, WG_SEM)
    wv_copy = local(wvs, wv_ref, WG_SEM + 1)
    wk_copy.start()
    wv_copy.start()
    for c in sent:
        c.wait_send()

    def drain(t, carry):
        tp_copy(t).wait_send()
        pp_copy(t).wait_send()
        pp_copy(t).wait_recv()
        return carry

    lax.fori_loop(0, TILES, drain, 0)
    for h in range(2):
        columns = pl.ds(h * GROUP * HD, GROUP * HD)
        local(dqs.at[:, columns], dq_ref.at[:, columns], DQ_SEM + h).wait()
    wk_copy.wait()
    wv_copy.wait()


def body(hidden_in, queries, out_grad, key_weight, value_weight, doc_lengths):
    any_space = pl.BlockSpec(memory_space=pl.ANY)
    bf16, f32 = jnp.bfloat16, jnp.float32
    block = (2, 2 * HD, SHARD)
    outs = pl.pallas_call(
        kernel,
        out_shape=(
            jax.ShapeDtypeStruct((ROWS, 2048), bf16),
            jax.ShapeDtypeStruct((ROWS, WIDTH // 2), bf16),
            jax.ShapeDtypeStruct((SHARD, 2 * HD), f32),
            jax.ShapeDtypeStruct((SHARD, 2 * HD), f32),
        ),
        in_specs=[any_space] * 5 + [pl.BlockSpec(memory_space=pltpu.SMEM)],
        out_specs=(any_space,) * 4,
        scratch_shapes=[
            pltpu.VMEM((ROWS, WIDTH), bf16),
            pltpu.VMEM((ROWS, 2048), bf16),
            pltpu.VMEM((ROWS, 2048), bf16),
            pltpu.VMEM((ROWS, 2048), bf16),
            pltpu.VMEM((2, 8, SHARD, 2 * HD), bf16),
            pltpu.VMEM((2, ROWS, 2 * HD), bf16),
            pltpu.VMEM((ROWS, 2 * HD), f32),
            pltpu.VMEM((4, 256, 128), f32),
            pltpu.VMEM((ROWS, 2 * HD), f32),
            pltpu.VMEM((2, ROWS, 2 * HD), bf16),
            pltpu.VMEM((2, 2 * HD, ROWS), bf16),
            pltpu.VMEM((2, 7, 2 * HD, SHARD), bf16),
            pltpu.VMEM(block, bf16),
            pltpu.VMEM(block, bf16),
            pltpu.VMEM(block, bf16),
            pltpu.VMEM((2, HD, SHARD), bf16),
            pltpu.VMEM((2, HD, SHARD), bf16),
            pltpu.VMEM(block, bf16),
            pltpu.VMEM(block, bf16),
            pltpu.VMEM(block, bf16),
            pltpu.VMEM((TILES, ROWS, TILE), bf16),
            pltpu.VMEM((TILES, ROWS, TILE), bf16),
            pltpu.VMEM((TILES, ROWS, TILE), bf16),
            pltpu.VMEM((SHARD, 2 * HD), f32),
            pltpu.VMEM((SHARD, 2 * HD), f32),
            pltpu.SemaphoreType.DMA((REMOTE_SEMS,)),
            pltpu.SemaphoreType.DMA((REMOTE_SEMS,)),
            pltpu.SemaphoreType.DMA((LOCAL_SEMS,)),
        ],
        compiler_params=pltpu.CompilerParams(
            collective_id=0, has_side_effects=True, vmem_limit_bytes=62 * 1024 * 1024
        ),
        cost_estimate=pl.CostEstimate(flops=18_000_000_000, bytes_accessed=24_000_000, transcendentals=2_100_000),
    )(hidden_in[0], queries[0], out_grad[0], key_weight[0], value_weight[0], doc_lengths[0])
    return tuple(out[None] for out in outs)


def solution(mesh):
    return jax.shard_map(
        body,
        mesh=mesh,
        in_specs=(
            P("pp", "dp", None),
            P("pp", "dp", "tp"),
            P("pp", "dp", "tp"),
            P("pp", "dp", "tp"),
            P("pp", "dp", "tp"),
            P("pp", "dp", None),
        ),
        out_specs=(
            P("pp", "dp", "tp"),
            P("pp", "dp", "tp"),
            P("pp", "dp", "tp"),
            P("pp", "dp", "tp"),
        ),
        check_vma=False,
    )
```

time: 525 us -> 219 us (0.42)
  waiting for transfers between devices: 414 us -> 0 us
  Pallas kernels: 0 us -> 210 us
  matrix products: 62.2 us -> 0 us
  local copies, waits for them, and re-layouts: 22.9 us -> 7.9 us
  between operations: 14 us -> 0.65 us
  other arithmetic: 6.37 us -> 0 us
  starting transfers between devices: 5.36 us -> 0 us
    reduce_scatter x2 -> x0, waiting for transfers between devices: 253 us -> none  [the longest x1 238 us: body(): lax.psum_scatter((product * grad_scale).astype(jnp.bfloat16), 'dp', scatt...]
    pallas_call x0 -> x1, Pallas kernels: none -> 210 us  [body(): pl.pallas_call(kernel, out_shape=(jax.ShapeDtypeStruct((ROWS, 2048), bf16...]
    all_gather x1 -> x0, waiting for transfers between devices: 161 us -> none  [body(): lax.all_gather(stacked, 'dp', axis=0, tiled=True)]
    dot_general x15 -> x0, matrix products: 62.2 us -> none  [the longest x1 10.7 us: body(): lax.dot_general(hidden_cols, joined_grad, (((0,), (0,)), ((), ())), prefe...]
    unnamed x17 -> x10, local copies, waits for them, and re-layouts: 16.1 us -> 7.9 us
  transfers between devices with their start and end apart: 4 -> 0, of which waited for: 3 -> 0; matrix products, arithmetic and copies ran while one was open for 7% -> 0% of each run, Pallas kernels for 0% -> 0%
where the time goes in v1:
time: 219 us
  Pallas kernels  210 us (96%)
  local copies, waits for them, and re-layouts  7.9 us (4%)
    pallas_call x1, Pallas kernels, body(): pl.pallas_call(kernel, out_shape=(jax.ShapeDtypeStruct((ROWS, 2048), bf16...  210 us
    unnamed x10, local copies, waits for them, and re-layouts  7.9 us

profile of v1, /device:TPU:1, one launch (start us, length us, event | category | flops | bytes accessed | tf_op | source)
XLA Modules:
  0.0 218.8 jit_solution(6795333488093276858)
XLA Ops:
  0.6 210.2 %shard_map.93 = (bf16[512,2048]{1,0:T(8,128)(2,1)}, bf16[512,4096]{1,0:T(8,128)(2,1)}, f32[1024,256]{1,0:T(8,128)}, f32[1024,256]{1,0:T(8,128)}) custom-call(bf16[512,8192]{1,0:T(8,128)(2,1)} %bitcast.14, bf16[512,2048]{1,0:T(8,128)(2,1)} %bitcast.15, bf16[512,2048]{1,0:T(8,128)(2,1)} %bitcast.16, bf16[1024,256]{1,0:T(8,128)(2,1)} %bitcast.17, ...), custom_call_target="tpu_custom_call" | custom-call | flops 17999998976 | bytes 24000000 | tf_op jit(solution)/shard_map/pallas_call | solution.py:370
  210.8 0.0 copy-start
  210.8 3.3 %copy.14 = bf16[1,512,2048]{2,1,0:T(8,128)(2,1)} copy(bf16[1,512,2048]{2,1,0:T(8,128)(2,1)} %bitcast.11) | data formatting | bytes 4194304
  214.2 0.0 copy-done
  214.2 0.0 copy-start.2
  214.2 2.0 copy.15
  216.2 0.0 copy-done.2
  216.2 0.0 copy-start.1
  216.2 1.0 copy.16
  217.2 0.6 copy-done.1
  217.8 1.0 copy.17
Async XLA Ops:
  210.8 3.3 %copy-start = (bf16[512,4096]{1,0:T(8,128)(2,1)S(1)}, bf16[512,4096]{1,0:T(8,128)(2,1)}, u32[]{:S(2)}) copy-start(bf16[512,4096]{1,0:T(8,128)(2,1)} %get-tuple-element.9) | copy-start | bytes 12582916
  214.2 2.0 copy-start.2
  216.2 1.6 copy-start.1

commit v2 on v1

--- a/solution.py
+++ b/solution.py
@@ -24,7 +24,14 @@
 PER_HEAD = len(GATHER) + len(SCATTER)
 TP_SEM = 2 * PER_HEAD
 PP_SEM = TP_SEM + TILES
-REMOTE_SEMS = PP_SEM + TILES
+HOP1_SEM = PP_SEM + TILES
+HOP2_SEM = HOP1_SEM + 2
+HOP3_SEM = HOP2_SEM + 2
+RELAY_SEM = HOP3_SEM + 2
+PASS_SEM = RELAY_SEM + 3
+REMOTE_SEMS = PASS_SEM + 3
+LONG_TILES = (1, 3)
+RELAY_TILES = (0, 4, 6)
 HID_SEM, Q_SEM, G_SEM, W_SEM, DQ_SEM, WG_SEM = 0, 8, 9, 10, 14, 16
 LOCAL_SEMS = 18
 
@@ -34,7 +41,7 @@
     dq_ref, lg_ref, wk_ref, wv_ref,
     hid, qs, gs, dqs, wg, kv, acc, bias, gacc, gkv, gkvt, prod,
     ry1, rp1, rm1, rp2, rm2, ry3, rp3, rm3,
-    lgs, lgr, lgo, wks, wvs, ssem, rsem, lsem,
+    lgs, lgr, lgo, hop1, hop2, held, wks, wvs, ssem, rsem, lsem,
 ):
     dp, pp, tp = lax.axis_index("dp"), lax.axis_index("pp"), lax.axis_index("tp")
     x, y = dp // 2, dp % 2
@@ -43,13 +50,19 @@
     j_q, j_pq, j_mq, j_2q = x * 2 + yq, xp * 2 + yq, xm * 2 + yq, x2 * 2 + yq
     dev_p, dev_m, dev_y = (j_p, pp, tp), (j_m, pp, tp), (j_q, pp, tp)
     dev_t = (dp, pp, 1 - tp)
-    dev_prev, dev_next = (dp, (pp + 7) % 8, tp), (dp, (pp + 1) % 8, tp)
+    hi, z = pp // 4, pp % 4
+    z_up, z_down = (z + 1) % 4, (z + 3) % 4
+    dev_prev = (dp, (pp + 7) % 8, tp)
+    dev_up, dev_down = (dp, hi * 4 + z_up, tp), (dp, hi * 4 + z_down, tp)
+    dev_far = (dp, (1 - hi) * 4 + z, tp)
+    dev_far_up, dev_far_down = (dp, (1 - hi) * 4 + z_up, tp), (dp, (1 - hi) * 4 + z_down, tp)
+    dev_hop3 = (dp, jnp.where(z == 2, 1 - hi, hi) * 4 + z_up, tp)
 
     sent = []
 
-    def remote(src, dst, k, dev):
+    def remote(src, dst, k, dev, arrival=None):
         return pltpu.make_async_remote_copy(
-            src_ref=src, dst_ref=dst, send_sem=ssem.at[k], recv_sem=rsem.at[k],
+            src_ref=src, dst_ref=dst, send_sem=ssem.at[k], recv_sem=rsem.at[k if arrival is None else arrival],
             device_id=dev, device_id_type=MESH,
         )
 
@@ -73,9 +86,9 @@
     g_copy.start()
 
     barrier = pltpu.get_barrier_semaphore()
-    for dev in (dev_p, dev_m, dev_y, dev_t, dev_prev, dev_next):
+    for dev in (dev_p, dev_m, dev_y, dev_t, dev_up, dev_down, dev_far, dev_far_up, dev_far_down):
         pl.semaphore_signal(barrier, inc=1, device_id=dev, device_id_type=MESH)
-    pl.semaphore_wait(barrier, 6)
+    pl.semaphore_wait(barrier, 9)
 
     def gather_copy(h, name):
         dev = {"p": dev_p, "m": dev_m, "y": dev_y}[name[0]]
@@ -214,9 +227,11 @@
         wks[:, pl.ds(h * HD, HD)] = total[:HD].T
         wvs[:, pl.ds(h * HD, HD)] = total[HD:].T
 
-    for c in w_copies:
+    for c in w_copies[:2]:
         c.wait()
-    gather_start(0, "p0a", "p0b", "m0a", "m0b", "y0a", "y0b")
+    gather_start(0, "p0a", "m0b", "y0a", "p0b", "m0a", "y0b")
+    for c in w_copies[2:]:
+        c.wait()
     ends, last = [], jnp.int32(0)
     for k in range(8):
         last = last + len_ref[0, k]
@@ -234,12 +249,11 @@
     for c in hid_copies:
         c.wait()
     project(0, j_me, True)
-    gather_wait(0, "p0a", "m0a")
-    gather_start(0, "p1a")
+    gather_wait(0, "p0a", "m0b")
+    gather_start(0, "p1a", "m1b")
     gather_wait(0, "y0a")
     gather_start(0, "p2a", "m2a")
-    gather_wait(0, "m0b")
-    gather_start(0, "m1b")
+    gather_wait(0, "m0a")
     gather_wait(0, "p0b", "y0b")
     gather_start(0, "p2b", "m2b")
     for j in (j_m, j_p, j_q):
@@ -250,7 +264,7 @@
     gather_start(0, "y2b")
     project(0, j_2)
     gather_wait(0, "p2a", "m2a")
-    gather_start(1, "p0a", "p0b", "m0a", "m0b")
+    gather_start(1, "p0a", "m0b", "p0b", "m0a")
     gather_wait(0, "y2a")
     gather_start(1, "y0a", "y0b")
     gather_wait(0, "p2b", "m2b")
@@ -264,13 +278,12 @@
 
     gacc[...] = jnp.zeros_like(gacc)
     attend(0, 0)
-    gather_wait(1, "p0a", "m0a")
-    gather_start(1, "p1a")
+    gather_wait(1, "p0a", "m0b")
+    gather_start(1, "p1a", "m1b")
     gather_wait(1, "y0a")
     gather_start(1, "p2a", "m2a")
     attend(0, 1)
-    gather_wait(1, "m0b")
-    gather_start(1, "m1b")
+    gather_wait(1, "m0a")
     gather_wait(1, "p0b", "y0b")
     gather_start(1, "p2b", "m2b")
     attend(0, 2)
@@ -298,7 +311,6 @@
     gacc[...] = jnp.zeros_like(gacc)
     attend(1, 0)
     attend(1, 1)
-    scatter_second(0)
     attend(1, 2)
     attend(1, 3)
     finish_head(1)
@@ -306,9 +318,56 @@
     def tp_copy(t):
         return remote(lgs.at[t], lgr.at[t], TP_SEM + t, dev_t)
 
+    def out_tile(t):
+        return lg_ref.at[:, pl.ds(pl.multiple_of(t * TILE, TILE), TILE)]
+
     def pp_copy(t):
-        columns = pl.ds(pl.multiple_of(t * TILE, TILE), TILE)
-        return remote(lgo.at[t], lg_ref.at[:, columns], PP_SEM + t, dev_prev)
+        return remote(lgo.at[t], out_tile(t), PP_SEM + t, dev_prev)
+
+    def relay_copy(i, t):
+        return remote(lgo.at[t], held.at[i], RELAY_SEM + i, dev_down)
+
+    def pass_copy(i, t):
+        return remote(held.at[i], out_tile(t), PASS_SEM + i, dev_far, PP_SEM + t)
+
+    def hop1_copy(i, t):
+        return remote(lgo.at[t], hop1.at[i], HOP1_SEM + i, dev_up)
+
+    def hop2_copy(i):
+        return remote(hop1.at[i], hop2.at[i], HOP2_SEM + i, dev_up)
+
+    def hop3_copy(i, t):
+        return remote(hop2.at[i], out_tile(t), HOP3_SEM + i, dev_hop3, PP_SEM + t)
+
+    def second_hop(i):
+        hop1_copy(i, LONG_TILES[i]).wait_recv()
+        hop2_copy(i).start()
+
+    def third_hop(i):
+        hop2_copy(i).wait_recv()
+        hop3_copy(i, LONG_TILES[i]).start()
+
+    def pass_on(i):
+        @pl.when(z == 3)
+        def _():
+            relay_copy(i, RELAY_TILES[i]).wait_recv()
+            pass_copy(i, RELAY_TILES[i]).start()
+
+    def send_tile(t):
+        is_long = (t == LONG_TILES[0]) | (t == LONG_TILES[1])
+        is_relay = (z == 0) & ((t == RELAY_TILES[0]) | (t == RELAY_TILES[1]) | (t == RELAY_TILES[2]))
+
+        @pl.when(is_long)
+        def _():
+            hop1_copy(t // 2, t).start()
+
+        @pl.when(is_relay)
+        def _():
+            relay_copy(jnp.maximum(t // 2 - 1, 0), t).start()
+
+        @pl.when(jnp.logical_not(is_long | is_relay))
+        def _():
+            pp_copy(t).start()
 
     def layer_tile(half, t):
         j = half * 4 + t // 2
@@ -328,34 +387,62 @@
         def _():
             tp_copy(t - 1).wait_recv()
             lgo[t - 1] = (wide(lgo[t - 1]) + wide(lgr[t - 1])).astype(jnp.bfloat16)
-            pp_copy(t - 1).start()
+            send_tile(t - 1)
 
         return carry
 
     lax.fori_loop(0, TILES + 1, layer_step, 0)
 
-    scatter_third(0)
+    scatter_second(0)
     terms(1, 0, 1, 2)
     scatter_start(1, "y1", "p1", "m1")
+    scatter_third(0)
+    scatter_rest_terms(1)
+    second_hop(0)
+    pass_on(0)
     scatter_last(0)
-    scatter_rest_terms(1)
     scatter_second(1)
+    second_hop(1)
     scatter_third(1)
+    third_hop(0)
+    pass_on(1)
     scatter_last(1)
     wk_copy = local(wks, wk_ref, WG_SEM)
     wv_copy = local(wvs, wv_ref, WG_SEM + 1)
     wk_copy.start()
     wv_copy.start()
+    third_hop(1)
+    pass_on(2)
     for c in sent:
         c.wait_send()
-
-    def drain(t, carry):
+    for t in range(TILES):
         tp_copy(t).wait_send()
-        pp_copy(t).wait_send()
+    for i, t in enumerate(LONG_TILES):
+        hop1_copy(i, t).wait_send()
+        hop2_copy(i).wait_send()
+        hop3_copy(i, t).wait_send()
+    for t in range(TILES):
+        if t in LONG_TILES:
+            continue
+        if t not in RELAY_TILES:
+            pp_copy(t).wait_send()
+            continue
+        i = RELAY_TILES.index(t)
+
+        @pl.when(z == 0)
+        def _(i=i, t=t):
+            relay_copy(i, t).wait_send()
+
+        @pl.when(z != 0)
+        def _(t=t):
+            pp_copy(t).wait_send()
+
+        @pl.when(z == 3)
+        def _(i=i, t=t):
+            pass_copy(i, t).wait_send()
+
+    for t in range(TILES):
         pp_copy(t).wait_recv()
-        return carry
-
-    lax.fori_loop(0, TILES, drain, 0)
     for h in range(2):
         columns = pl.ds(h * GROUP * HD, GROUP * HD)
         local(dqs.at[:, columns], dq_ref.at[:, columns], DQ_SEM + h).wait()
@@ -401,6 +488,9 @@
             pltpu.VMEM((TILES, ROWS, TILE), bf16),
             pltpu.VMEM((TILES, ROWS, TILE), bf16),
             pltpu.VMEM((TILES, ROWS, TILE), bf16),
+            pltpu.VMEM((2, ROWS, TILE), bf16),
+            pltpu.VMEM((2, ROWS, TILE), bf16),
+            pltpu.VMEM((3, ROWS, TILE), bf16),
             pltpu.VMEM((SHARD, 2 * HD), f32),
             pltpu.VMEM((SHARD, 2 * HD), f32),
             pltpu.SemaphoreType.DMA((REMOTE_SEMS,)),

time: 219 us -> 189 us (0.86)
  Pallas kernels: 210 us -> 180 us
    pallas_call x1, Pallas kernels: 210 us -> 180 us  [body(): pl.pallas_call(kernel, out_shape=(jax.ShapeDtypeStruct((ROWS, 2048), bf16...]
where the time goes in v2:
time: 189 us
  Pallas kernels  180 us (95%)
  local copies, waits for them, and re-layouts  7.9 us (4%)
    pallas_call x1, Pallas kernels, body(): pl.pallas_call(kernel, out_shape=(jax.ShapeDtypeStruct((ROWS, 2048), bf16...  180 us
    unnamed x10, local copies, waits for them, and re-layouts  7.9 us

profile of v2, /device:TPU:1, one launch (start us, length us, event | category | flops | bytes accessed | tf_op | source)
XLA Modules:
  0.0 188.9 jit_solution(15643787829188787679)
XLA Ops:
  0.6 180.3 %shard_map.93 = (bf16[512,2048]{1,0:T(8,128)(2,1)}, bf16[512,4096]{1,0:T(8,128)(2,1)}, f32[1024,256]{1,0:T(8,128)}, f32[1024,256]{1,0:T(8,128)}) custom-call(bf16[512,8192]{1,0:T(8,128)(2,1)} %bitcast.14, bf16[512,2048]{1,0:T(8,128)(2,1)} %bitcast.15, bf16[512,2048]{1,0:T(8,128)(2,1)} %bitcast.16, bf16[1024,256]{1,0:T(8,128)(2,1)} %bitcast.17, ...), custom_call_target="tpu_custom_call" | custom-call | flops 17999998976 | bytes 24000000 | tf_op jit(solution)/shard_map/pallas_call | solution.py:457
  181.0 0.0 copy-start
  181.0 3.3 %copy.14 = bf16[1,512,2048]{2,1,0:T(8,128)(2,1)} copy(bf16[1,512,2048]{2,1,0:T(8,128)(2,1)} %bitcast.11) | data formatting | bytes 4194304
  184.3 0.0 copy-done
  184.3 0.0 copy-start.2
  184.3 2.0 %copy.15 = bf16[1,512,4096]{2,1,0:T(8,128)(2,1)} copy(bf16[1,512,4096]{2,1,0:T(8,128)(2,1)S(1)} %bitcast.10) | data formatting | bytes 8388608
  186.3 0.0 copy-done.2
  186.3 0.0 copy-start.1
  186.3 1.0 copy.16
  187.3 0.6 copy-done.1
  187.9 1.0 copy.17
Async XLA Ops:
  181.0 3.3 %copy-start = (bf16[512,4096]{1,0:T(8,128)(2,1)S(1)}, bf16[512,4096]{1,0:T(8,128)(2,1)}, u32[]{:S(2)}) copy-start(bf16[512,4096]{1,0:T(8,128)(2,1)} %get-tuple-element.9) | copy-start | bytes 12582916
  184.3 2.0 %copy-start.2 = (f32[1024,256]{1,0:T(8,128)S(1)}, f32[1024,256]{1,0:T(8,128)}, u32[]{:S(2)}) copy-start(f32[1024,256]{1,0:T(8,128)} %get-tuple-element.10) | copy-start | bytes 3145732
  186.3 1.6 copy-start.1

commit v3 on v2

--- a/solution.py
+++ b/solution.py
@@ -31,7 +31,8 @@
 PASS_SEM = RELAY_SEM + 3
 REMOTE_SEMS = PASS_SEM + 3
 LONG_TILES = (1, 3)
-RELAY_TILES = (0, 4, 6)
+RELAY_TILES = (0, 2, 4)
+DIRECT_TILES = (5, 6, 7)
 HID_SEM, Q_SEM, G_SEM, W_SEM, DQ_SEM, WG_SEM = 0, 8, 9, 10, 14, 16
 LOCAL_SEMS = 18
 
@@ -363,9 +364,9 @@
 
         @pl.when(is_relay)
         def _():
-            relay_copy(jnp.maximum(t // 2 - 1, 0), t).start()
-
-        @pl.when(jnp.logical_not(is_long | is_relay))
+            relay_copy(t // 2, t).start()
+
+        @pl.when(jnp.logical_not(is_long | (z == 0)))
         def _():
             pp_copy(t).start()
 
@@ -392,6 +393,14 @@
         return carry
 
     lax.fori_loop(0, TILES + 1, layer_step, 0)
+
+    def release():
+        @pl.when(z == 0)
+        def _():
+            relay_copy(1, RELAY_TILES[1]).wait_send()
+            for t in DIRECT_TILES:
+                pp_copy(t).start()
+
 
     scatter_second(0)
     terms(1, 0, 1, 2)
@@ -403,16 +412,17 @@
     scatter_last(0)
     scatter_second(1)
     second_hop(1)
+    release()
+    pass_on(1)
     scatter_third(1)
     third_hop(0)
-    pass_on(1)
+    pass_on(2)
     scatter_last(1)
     wk_copy = local(wks, wk_ref, WG_SEM)
     wv_copy = local(wvs, wv_ref, WG_SEM + 1)
     wk_copy.start()
     wv_copy.start()
     third_hop(1)
-    pass_on(2)
     for c in sent:
         c.wait_send()
     for t in range(TILES):
@@ -431,7 +441,8 @@
 
         @pl.when(z == 0)
         def _(i=i, t=t):
-            relay_copy(i, t).wait_send()
+            if i != 1:
+                relay_copy(i, t).wait_send()
 
         @pl.when(z != 0)
         def _(t=t):

time: 189 us -> 178 us (0.942)
  Pallas kernels: 180 us -> 169 us
    pallas_call x1, Pallas kernels: 180 us -> 169 us  [body(): pl.pallas_call(kernel, out_shape=(jax.ShapeDtypeStruct((ROWS, 2048), bf16...]
where the time goes in v3:
time: 178 us
  Pallas kernels  169 us (95%)
  local copies, waits for them, and re-layouts  7.9 us (4%)
    pallas_call x1, Pallas kernels, body(): pl.pallas_call(kernel, out_shape=(jax.ShapeDtypeStruct((ROWS, 2048), bf16...  169 us
    unnamed x10, local copies, waits for them, and re-layouts  7.9 us

profile of v3, /device:TPU:1, one launch (start us, length us, event | category | flops | bytes accessed | tf_op | source)
XLA Modules:
  0.0 177.9 jit_solution(12850288749357873617)
XLA Ops:
  0.6 169.4 %shard_map.93 = (bf16[512,2048]{1,0:T(8,128)(2,1)}, bf16[512,4096]{1,0:T(8,128)(2,1)}, f32[1024,256]{1,0:T(8,128)}, f32[1024,256]{1,0:T(8,128)}) custom-call(bf16[512,8192]{1,0:T(8,128)(2,1)} %bitcast.14, bf16[512,2048]{1,0:T(8,128)(2,1)} %bitcast.15, bf16[512,2048]{1,0:T(8,128)(2,1)} %bitcast.16, bf16[1024,256]{1,0:T(8,128)(2,1)} %bitcast.17, ...), custom_call_target="tpu_custom_call" | custom-call | flops 17999998976 | bytes 24000000 | tf_op jit(solution)/shard_map/pallas_call | solution.py:468
  170.0 0.0 copy-start
  170.0 3.3 %copy.14 = bf16[1,512,2048]{2,1,0:T(8,128)(2,1)} copy(bf16[1,512,2048]{2,1,0:T(8,128)(2,1)} %bitcast.11) | data formatting | bytes 4194304
  173.3 0.0 copy-done
  173.3 0.0 copy-start.2
  173.3 2.0 %copy.15 = bf16[1,512,4096]{2,1,0:T(8,128)(2,1)} copy(bf16[1,512,4096]{2,1,0:T(8,128)(2,1)S(1)} %bitcast.10) | data formatting | bytes 8388608
  175.3 0.0 copy-done.2
  175.3 0.0 copy-start.1
  175.3 1.0 copy.16
  176.3 0.6 copy-done.1
  176.9 1.0 copy.17
Async XLA Ops:
  170.0 3.3 %copy-start = (bf16[512,4096]{1,0:T(8,128)(2,1)S(1)}, bf16[512,4096]{1,0:T(8,128)(2,1)}, u32[]{:S(2)}) copy-start(bf16[512,4096]{1,0:T(8,128)(2,1)} %get-tuple-element.9) | copy-start | bytes 12582916
  173.3 2.0 %copy-start.2 = (f32[1024,256]{1,0:T(8,128)S(1)}, f32[1024,256]{1,0:T(8,128)}, u32[]{:S(2)}) copy-start(f32[1024,256]{1,0:T(8,128)} %get-tuple-element.10) | copy-start | bytes 3145732
  175.3 1.6 copy-start.1

commit v4 on v3

--- a/solution.py
+++ b/solution.py
@@ -20,7 +20,7 @@
 TN = (((0,), (0,)), ((), ()))
 
 GATHER = ("p0a", "p0b", "m0a", "m0b", "y0a", "y0b", "p1a", "m1b", "p2a", "p2b", "m2a", "m2b", "y2a", "y2b")
-SCATTER = ("y1", "p1", "m1", "p2", "m2", "y3", "p3k", "p3v", "m3k", "m3v")
+SCATTER = ("p2q", "m2q", "p1k", "p1v", "m1k", "m1v", "p2", "m2", "y3", "p3k", "p3v", "m3k", "m3v")
 PER_HEAD = len(GATHER) + len(SCATTER)
 TP_SEM = 2 * PER_HEAD
 PP_SEM = TP_SEM + TILES
@@ -41,7 +41,7 @@
     hidden_ref, query_ref, grad_ref, kw_ref, vw_ref, len_ref,
     dq_ref, lg_ref, wk_ref, wv_ref,
     hid, qs, gs, dqs, wg, kv, acc, bias, gacc, gkv, gkvt, prod,
-    ry1, rp1, rm1, rp2, rm2, ry3, rp3, rm3,
+    rp2q, rm2q, rp1, rm1, rp2, rm2, ry3, rp3, rm3,
     lgs, lgr, lgo, hop1, hop2, held, wks, wvs, ssem, rsem, lsem,
 ):
     dp, pp, tp = lax.axis_index("dp"), lax.axis_index("pp"), lax.axis_index("tp")
@@ -115,6 +115,11 @@
             acc[...] = term
         else:
             acc[...] += term
+
+    def project_half(h, j, half):
+        columns = pl.ds(pl.multiple_of(j * SHARD + half * HALF, HALF), HALF)
+        block = wg[h, j, pl.ds(half * HALF, HALF)]
+        acc[...] += jnp.dot(hid[:, columns], block, preferred_element_type=jnp.float32)
 
     def attend(h, b):
         w0 = 128 * max(b - 1, 0)
@@ -172,9 +177,12 @@
 
     def scatter_copy(h, name):
         src, dst, dev = {
-            "y1": (prod.at[h, 0], ry1.at[h], dev_y),
-            "p1": (prod.at[h, 1], rp1.at[h], dev_p),
-            "m1": (prod.at[h, 2], rm1.at[h], dev_m),
+            "p2q": (prod.at[h, 0, krows], rp2q.at[h], dev_p),
+            "m2q": (prod.at[h, 0, vrows], rm2q.at[h], dev_m),
+            "p1k": (prod.at[h, 1, krows], rp1.at[h, krows], dev_p),
+            "p1v": (prod.at[h, 1, vrows], rp1.at[h, vrows], dev_p),
+            "m1k": (prod.at[h, 2, krows], rm1.at[h, krows], dev_m),
+            "m1v": (prod.at[h, 2, vrows], rm1.at[h, vrows], dev_m),
             "p2": (prod.at[h, 3, krows], rp2.at[h], dev_p),
             "m2": (prod.at[h, 3, vrows], rm2.at[h], dev_m),
             "y3": (prod.at[h, 4], ry3.at[h], dev_y),
@@ -198,28 +206,32 @@
     def wide(block):
         return block.astype(jnp.float32)
 
+    def add(h, n, rows, *arrived):
+        total = wide(prod[h, n, rows])
+        for block in arrived:
+            total = total + wide(block)
+        prod[h, n, rows] = total.astype(jnp.bfloat16)
+
     def scatter_first(h):
-        terms(h, 0, 1, 2)
-        scatter_start(h, "y1", "p1", "m1")
-
-    def scatter_rest_terms(h):
-        terms(h, 3, 4, 5, 6)
-        scatter_start(h, "p3v", "m3k")
+        scatter_start(h, "p2q", "m2q", "p1v", "m1k", "p2", "m2")
 
     def scatter_second(h):
-        scatter_wait(h, "y1")
-        prod[h, 3] = (wide(prod[h, 3]) + wide(ry1[h])).astype(jnp.bfloat16)
-        scatter_start(h, "p2", "m2")
-        scatter_wait(h, "p1", "m1")
-        prod[h, 4] = (wide(prod[h, 4]) + wide(rp1[h]) + wide(rm1[h])).astype(jnp.bfloat16)
+        scatter_wait(h, "p2q", "m2q")
+        add(h, 1, krows, rp2q[h])
+        scatter_start(h, "p1k")
+        add(h, 2, vrows, rm2q[h])
+        scatter_start(h, "m1v")
+        scatter_wait(h, "p2", "m2")
+        add(h, 5, krows, rp2[h])
+        scatter_start(h, "p3k")
+        add(h, 6, vrows, rm2[h])
+        scatter_start(h, "m3v")
+
+    def scatter_third(h):
+        scatter_wait(h, "p1k", "p1v", "m1k", "m1v")
+        add(h, 4, krows, rp1[h, krows], rm1[h, krows])
+        add(h, 4, vrows, rp1[h, vrows], rm1[h, vrows])
         scatter_start(h, "y3")
-
-    def scatter_third(h):
-        scatter_wait(h, "p2", "m2")
-        prod[h, 5, krows] = (wide(prod[h, 5, krows]) + wide(rp2[h])).astype(jnp.bfloat16)
-        scatter_start(h, "p3k")
-        prod[h, 6, vrows] = (wide(prod[h, 6, vrows]) + wide(rm2[h])).astype(jnp.bfloat16)
-        scatter_start(h, "m3v")
 
     def scatter_last(h):
         own = term(h, j_me)
@@ -294,20 +306,23 @@
     gather_start(1, "y2b")
     attend(0, 3)
     finish_head(0)
-    terms(0, 0, 1, 2)
+    terms(0, 0, 1, 2, 3)
     project(1, j_me, True)
     for j in (j_m, j_p, j_q, j_2):
         project(1, j)
+    terms(0, 4, 5, 6)
     gather_wait(1, "p2a", "m2a", "y2a")
-    scatter_start(0, "y1", "p1", "m1")
-    terms(0, 3, 4, 5, 6)
+    scatter_first(0)
+    scatter_start(0, "p3v", "m3k")
+    project_half(1, j_pq, 0)
+    project_half(1, j_mq, 0)
+    project_half(1, j_2q, 0)
     gather_wait(1, "p2b", "m2b")
-    project(1, j_pq)
-    project(1, j_mq)
+    project_half(1, j_pq, 1)
+    project_half(1, j_mq, 1)
     gather_wait(1, "y2b")
-    project(1, j_2q)
+    project_half(1, j_2q, 1)
     kv[1] = acc[...].astype(jnp.bfloat16)
-    scatter_start(0, "p3v", "m3k")
 
     gacc[...] = jnp.zeros_like(gacc)
     attend(1, 0)
@@ -366,7 +381,7 @@
         def _():
             relay_copy(t // 2, t).start()
 
-        @pl.when(jnp.logical_not(is_long | (z == 0)))
+        @pl.when(jnp.logical_not(is_long) & ((z != 0) | (t == DIRECT_TILES[0])))
         def _():
             pp_copy(t).start()
 
@@ -398,31 +413,32 @@
         @pl.when(z == 0)
         def _():
             relay_copy(1, RELAY_TILES[1]).wait_send()
-            for t in DIRECT_TILES:
+            for t in DIRECT_TILES[1:]:
                 pp_copy(t).start()
 
 
     scatter_second(0)
-    terms(1, 0, 1, 2)
-    scatter_start(1, "y1", "p1", "m1")
+    terms(1, 0, 1, 2, 3)
+    scatter_first(1)
+    terms(1, 4, 5, 6)
+    scatter_start(1, "p3v", "m3k")
+    second_hop(0)
     scatter_third(0)
-    scatter_rest_terms(1)
-    second_hop(0)
     pass_on(0)
+    second_hop(1)
     scatter_last(0)
     scatter_second(1)
-    second_hop(1)
+    pass_on(1)
     release()
-    pass_on(1)
-    scatter_third(1)
     third_hop(0)
     pass_on(2)
+    scatter_third(1)
+    third_hop(1)
     scatter_last(1)
     wk_copy = local(wks, wk_ref, WG_SEM)
     wv_copy = local(wvs, wv_ref, WG_SEM + 1)
     wk_copy.start()
     wv_copy.start()
-    third_hop(1)
     for c in sent:
         c.wait_send()
     for t in range(TILES):
@@ -488,7 +504,8 @@
             pltpu.VMEM((2, ROWS, 2 * HD), bf16),
             pltpu.VMEM((2, 2 * HD, ROWS), bf16),
             pltpu.VMEM((2, 7, 2 * HD, SHARD), bf16),
-            pltpu.VMEM(block, bf16),
+            pltpu.VMEM((2, HD, SHARD), bf16),
+            pltpu.VMEM((2, HD, SHARD), bf16),
             pltpu.VMEM(block, bf16),
             pltpu.VMEM(block, bf16),
             pltpu.VMEM((2, HD, SHARD), bf16),

time: 178 us -> 185 us (1.039)
  the two profiles are of different devices: /device:TPU:1 before, /device:TPU:96 now
where the time goes in v4:
time: 185 us
  Pallas kernels  176 us (95%)
  local copies, waits for them, and re-layouts  7.9 us (4%)
    pallas_call x1, Pallas kernels, body(): pl.pallas_call(kernel, out_shape=(jax.ShapeDtypeStruct((ROWS, 2048), bf16...  176 us
    unnamed x10, local copies, waits for them, and re-layouts  7.9 us

profile of v4, /device:TPU:96, one launch (start us, length us, event | category | flops | bytes accessed | tf_op | source)
XLA Modules:
  0.0 185.0 jit_solution(2628822868490175104)
XLA Ops:
  0.6 176.4 %shard_map.93 = (bf16[512,2048]{1,0:T(8,128)(2,1)}, bf16[512,4096]{1,0:T(8,128)(2,1)}, f32[1024,256]{1,0:T(8,128)}, f32[1024,256]{1,0:T(8,128)}) custom-call(bf16[512,8192]{1,0:T(8,128)(2,1)} %bitcast.14, bf16[512,2048]{1,0:T(8,128)(2,1)} %bitcast.15, bf16[512,2048]{1,0:T(8,128)(2,1)} %bitcast.16, bf16[1024,256]{1,0:T(8,128)(2,1)} %bitcast.17, ...), custom_call_target="tpu_custom_call" | custom-call | flops 17999998976 | bytes 24000000 | tf_op jit(solution)/shard_map/pallas_call | solution.py:484
  177.1 0.0 copy-start
  177.1 3.3 %copy.14 = bf16[1,512,2048]{2,1,0:T(8,128)(2,1)} copy(bf16[1,512,2048]{2,1,0:T(8,128)(2,1)} %bitcast.11) | data formatting | bytes 4194304
  180.4 0.0 copy-done
  180.4 0.0 copy-start.2
  180.4 2.0 %copy.15 = bf16[1,512,4096]{2,1,0:T(8,128)(2,1)} copy(bf16[1,512,4096]{2,1,0:T(8,128)(2,1)S(1)} %bitcast.10) | data formatting | bytes 8388608
  182.4 0.0 copy-done.2
  182.4 0.0 copy-start.1
  182.4 1.0 copy.16
  183.4 0.6 copy-done.1
  184.0 1.0 copy.17
Async XLA Ops:
  177.1 3.3 %copy-start = (bf16[512,4096]{1,0:T(8,128)(2,1)S(1)}, bf16[512,4096]{1,0:T(8,128)(2,1)}, u32[]{:S(2)}) copy-start(bf16[512,4096]{1,0:T(8,128)(2,1)} %get-tuple-element.9) | copy-start | bytes 12582916
  180.4 2.0 %copy-start.2 = (f32[1024,256]{1,0:T(8,128)S(1)}, f32[1024,256]{1,0:T(8,128)}, u32[]{:S(2)}) copy-start(f32[1024,256]{1,0:T(8,128)} %get-tuple-element.10) | copy-start | bytes 3145732
  182.4 1.6 copy-start.1

commit v5 on v4

--- a/solution.py
+++ b/solution.py
@@ -40,9 +40,9 @@
 def kernel(
     hidden_ref, query_ref, grad_ref, kw_ref, vw_ref, len_ref,
     dq_ref, lg_ref, wk_ref, wv_ref,
-    hid, qs, gs, dqs, wg, kv, acc, bias, gacc, gkv, gkvt, prod,
+    hid, qs, gs, wg, kv, acc, bias, gacc, gkv, gkvt, prod,
     rp2q, rm2q, rp1, rm1, rp2, rm2, ry3, rp3, rm3,
-    lgs, lgr, lgo, hop1, hop2, held, wks, wvs, ssem, rsem, lsem,
+    lgs, lgr, lgo, hop1, hop2, held, ssem, rsem, lsem,
 ):
     dp, pp, tp = lax.axis_index("dp"), lax.axis_index("pp"), lax.axis_index("tp")
     x, y = dp // 2, dp % 2
@@ -144,8 +144,8 @@
             ds = (p * (dpr - delta)).astype(jnp.bfloat16)
             dq = lax.dot_general(ds, keys, TN, preferred_element_type=jnp.float32) * (HD ** -0.5)
             dq = dq.astype(jnp.bfloat16)
-            dqs[rows, pl.ds(c0, HD)] = dq[:128]
-            dqs[rows, pl.ds(c0 + HD, HD)] = dq[128:]
+            dq_ref[rows, pl.ds(c0, HD)] = dq[:128]
+            dq_ref[rows, pl.ds(c0 + HD, HD)] = dq[128:]
             gacc[window, pl.ds(0, HD)] += jnp.dot(ds, q2, preferred_element_type=jnp.float32)
             gacc[window, pl.ds(HD, HD)] += jnp.dot(low, g2, preferred_element_type=jnp.float32)
             return carry
@@ -154,7 +154,6 @@
 
     def finish_head(h):
         columns = pl.ds(h * GROUP * HD, GROUP * HD)
-        local(dqs.at[:, columns], dq_ref.at[:, columns], DQ_SEM + h).start()
         key_part = gacc[:, pl.ds(0, HD)] * (HD ** -0.5)
         value_part = gacc[:, pl.ds(HD, HD)]
         gkv[h, :, pl.ds(0, HD)] = key_part.astype(jnp.bfloat16)
@@ -237,8 +236,8 @@
         own = term(h, j_me)
         scatter_wait(h, "y3", "p3k", "p3v", "m3k", "m3v")
         total = wide(own) + wide(ry3[h]) + wide(rp3[h]) + wide(rm3[h])
-        wks[:, pl.ds(h * HD, HD)] = total[:HD].T
-        wvs[:, pl.ds(h * HD, HD)] = total[HD:].T
+        wk_ref[:, pl.ds(h * HD, HD)] = total[:HD].T
+        wv_ref[:, pl.ds(h * HD, HD)] = total[HD:].T
 
     for c in w_copies[:2]:
         c.wait()
@@ -409,13 +408,12 @@
 
     lax.fori_loop(0, TILES + 1, layer_step, 0)
 
-    def release():
+    def release(t, wait):
         @pl.when(z == 0)
         def _():
-            relay_copy(1, RELAY_TILES[1]).wait_send()
-            for t in DIRECT_TILES[1:]:
-                pp_copy(t).start()
-
+            if wait:
+                relay_copy(1, RELAY_TILES[1]).wait_send()
+            pp_copy(t).start()
 
     scatter_second(0)
     terms(1, 0, 1, 2, 3)
@@ -428,17 +426,14 @@
     second_hop(1)
     scatter_last(0)
     scatter_second(1)
+    release(DIRECT_TILES[1], True)
     pass_on(1)
-    release()
     third_hop(0)
+    scatter_third(1)
+    release(DIRECT_TILES[2], False)
+    third_hop(1)
     pass_on(2)
-    scatter_third(1)
-    third_hop(1)
     scatter_last(1)
-    wk_copy = local(wks, wk_ref, WG_SEM)
-    wv_copy = local(wvs, wv_ref, WG_SEM + 1)
-    wk_copy.start()
-    wv_copy.start()
     for c in sent:
         c.wait_send()
     for t in range(TILES):
@@ -470,30 +465,25 @@
 
     for t in range(TILES):
         pp_copy(t).wait_recv()
-    for h in range(2):
-        columns = pl.ds(h * GROUP * HD, GROUP * HD)
-        local(dqs.at[:, columns], dq_ref.at[:, columns], DQ_SEM + h).wait()
-    wk_copy.wait()
-    wv_copy.wait()
 
 
 def body(hidden_in, queries, out_grad, key_weight, value_weight, doc_lengths):
     any_space = pl.BlockSpec(memory_space=pl.ANY)
+    vmem_space = pl.BlockSpec(memory_space=pltpu.VMEM)
     bf16, f32 = jnp.bfloat16, jnp.float32
     block = (2, 2 * HD, SHARD)
     outs = pl.pallas_call(
         kernel,
         out_shape=(
-            jax.ShapeDtypeStruct((ROWS, 2048), bf16),
+            pltpu.VMEM((ROWS, 2048), bf16),
             jax.ShapeDtypeStruct((ROWS, WIDTH // 2), bf16),
-            jax.ShapeDtypeStruct((SHARD, 2 * HD), f32),
-            jax.ShapeDtypeStruct((SHARD, 2 * HD), f32),
+            pltpu.VMEM((SHARD, 2 * HD), f32),
+            pltpu.VMEM((SHARD, 2 * HD), f32),
         ),
         in_specs=[any_space] * 5 + [pl.BlockSpec(memory_space=pltpu.SMEM)],
-        out_specs=(any_space,) * 4,
+        out_specs=(vmem_space, any_space, vmem_space, vmem_space),
         scratch_shapes=[
             pltpu.VMEM((ROWS, WIDTH), bf16),
-            pltpu.VMEM((ROWS, 2048), bf16),
             pltpu.VMEM((ROWS, 2048), bf16),
             pltpu.VMEM((ROWS, 2048), bf16),
             pltpu.VMEM((2, 8, SHARD, 2 * HD), bf16),
@@ -519,14 +509,12 @@
             pltpu.VMEM((2, ROWS, TILE), bf16),
             pltpu.VMEM((2, ROWS, TILE), bf16),
             pltpu.VMEM((3, ROWS, TILE), bf16),
-            pltpu.VMEM((SHARD, 2 * HD), f32),
-            pltpu.VMEM((SHARD, 2 * HD), f32),
             pltpu.SemaphoreType.DMA((REMOTE_SEMS,)),
             pltpu.SemaphoreType.DMA((REMOTE_SEMS,)),
             pltpu.SemaphoreType.DMA((LOCAL_SEMS,)),
         ],
         compiler_params=pltpu.CompilerParams(
-            collective_id=0, has_side_effects=True, vmem_limit_bytes=62 * 1024 * 1024
+            collective_id=0, has_side_effects=True, vmem_limit_bytes=56 * 1024 * 1024
         ),
         cost_estimate=pl.CostEstimate(flops=18_000_000_000, bytes_accessed=24_000_000, transcendentals=2_100_000),
     )(hidden_in[0], queries[0], out_grad[0], key_weight[0], value_weight[0], doc_lengths[0])

time: 185 us -> 163 us (0.88)
  the two profiles are of different devices: /device:TPU:96 before, /device:TPU:1 now
where the time goes in v5:
time: 163 us
  Pallas kernels  156 us (96%)
  local copies, waits for them, and re-layouts  6.28 us (4%)
    pallas_call x1, Pallas kernels, body(): pl.pallas_call(kernel, out_shape=(pltpu.VMEM((ROWS, 2048), bf16), jax.Sha...  156 us
    unnamed x6, local copies, waits for them, and re-layouts  6.28 us

profile of v5, /device:TPU:1, one launch (start us, length us, event | category | flops | bytes accessed | tf_op | source)
XLA Modules:
  0.0 162.9 jit_solution(9323693303321812397)
XLA Ops:
  0.6 156.0 %shard_map.93 = (bf16[512,2048]{1,0:T(8,128)(2,1)S(1)}, bf16[512,4096]{1,0:T(8,128)(2,1)}, f32[1024,256]{1,0:T(8,128)S(1)}, f32[1024,256]{1,0:T(8,128)S(1)}) custom-call(bf16[512,8192]{1,0:T(8,128)(2,1)} %bitcast.14, bf16[512,2048]{1,0:T(8,128)(2,1)} %bitcast.15, bf16[512,2048]{1,0:T(8,128)(2,1)} %bitcast.16, bf16[1024,256]{1,0:T(8,128)(2,1)} %bitcast.17, ...), custom_call_target="tpu_custom_call" | custom-call | flops 17999998976 | bytes 24000000 | tf_op jit(solution)/shard_map/pallas_call | solution.py:475
  156.6 1.3 copy.14
  158.0 0.0 copy-start
  158.0 1.0 copy.15
  158.9 1.0 copy.16
  159.9 1.0 copy-done
  160.9 2.0 %copy.17 = bf16[1,512,4096]{2,1,0:T(8,128)(2,1)} copy(bf16[1,512,4096]{2,1,0:T(8,128)(2,1)S(1)} %bitcast.13) | data formatting | bytes 8388608
Async XLA Ops:
  158.0 2.9 %copy-start = (bf16[512,4096]{1,0:T(8,128)(2,1)S(1)}, bf16[512,4096]{1,0:T(8,128)(2,1)}, u32[]{:S(2)}) copy-start(bf16[512,4096]{1,0:T(8,128)(2,1)} %get-tuple-element.9) | copy-start | bytes 12582916

commit v6 on v5

--- a/solution.py
+++ b/solution.py
@@ -33,8 +33,8 @@
 LONG_TILES = (1, 3)
 RELAY_TILES = (0, 2, 4)
 DIRECT_TILES = (5, 6, 7)
-HID_SEM, Q_SEM, G_SEM, W_SEM, DQ_SEM, WG_SEM = 0, 8, 9, 10, 14, 16
-LOCAL_SEMS = 18
+HID_SEM, Q_SEM, G_SEM, W_SEM = 0, 8, 9, 10
+LOCAL_SEMS = 14
 
 
 def kernel(
@@ -150,7 +150,7 @@
             gacc[window, pl.ds(HD, HD)] += jnp.dot(low, g2, preferred_element_type=jnp.float32)
             return carry
 
-        lax.fori_loop(0, GROUP // 2, pair, 0)
+        lax.fori_loop(0, GROUP // 2, pair, 0, unroll=4)
 
     def finish_head(h):
         columns = pl.ds(h * GROUP * HD, GROUP * HD)
@@ -158,8 +158,10 @@
         value_part = gacc[:, pl.ds(HD, HD)]
         gkv[h, :, pl.ds(0, HD)] = key_part.astype(jnp.bfloat16)
         gkv[h, :, pl.ds(HD, HD)] = value_part.astype(jnp.bfloat16)
-        gkvt[h, pl.ds(0, HD), :] = key_part.T.astype(jnp.bfloat16)
-        gkvt[h, pl.ds(HD, HD), :] = value_part.T.astype(jnp.bfloat16)
+
+    def flip_head(h):
+        gkvt[h, pl.ds(0, HD), :] = (gacc[:, pl.ds(0, HD)] * (HD ** -0.5)).T.astype(jnp.bfloat16)
+        gkvt[h, pl.ds(HD, HD), :] = gacc[:, pl.ds(HD, HD)].T.astype(jnp.bfloat16)
 
     targets = (j_2q, j_pq, j_mq, j_2, j_q, j_p, j_m)
 
@@ -305,6 +307,7 @@
     gather_start(1, "y2b")
     attend(0, 3)
     finish_head(0)
+    flip_head(0)
     terms(0, 0, 1, 2, 3)
     project(1, j_me, True)
     for j in (j_m, j_p, j_q, j_2):
@@ -331,7 +334,7 @@
     finish_head(1)
 
     def tp_copy(t):
-        return remote(lgs.at[t], lgr.at[t], TP_SEM + t, dev_t)
+        return remote(lgs.at[t % 2], lgr.at[t], TP_SEM + t, dev_t)
 
     def out_tile(t):
         return lg_ref.at[:, pl.ds(pl.multiple_of(t * TILE, TILE), TILE)]
@@ -392,9 +395,13 @@
         )
 
     def layer_step(t, carry):
+        @pl.when((t >= 2) & (t < TILES))
+        def _():
+            tp_copy(t - 2).wait_send()
+
         @pl.when(t < TILES)
         def _():
-            lgs[t] = layer_tile(1 - tp, t).astype(jnp.bfloat16)
+            lgs[t % 2] = layer_tile(1 - tp, t).astype(jnp.bfloat16)
             tp_copy(t).start()
             lgo[t] = layer_tile(tp, t).astype(jnp.bfloat16)
 
@@ -416,6 +423,7 @@
             pp_copy(t).start()
 
     scatter_second(0)
+    flip_head(1)
     terms(1, 0, 1, 2, 3)
     scatter_first(1)
     terms(1, 4, 5, 6)
@@ -436,7 +444,7 @@
     scatter_last(1)
     for c in sent:
         c.wait_send()
-    for t in range(TILES):
+    for t in range(TILES - 2, TILES):
         tp_copy(t).wait_send()
     for i, t in enumerate(LONG_TILES):
         hop1_copy(i, t).wait_send()
@@ -476,12 +484,12 @@
         kernel,
         out_shape=(
             pltpu.VMEM((ROWS, 2048), bf16),
-            jax.ShapeDtypeStruct((ROWS, WIDTH // 2), bf16),
+            pltpu.VMEM((ROWS, WIDTH // 2), bf16),
             pltpu.VMEM((SHARD, 2 * HD), f32),
             pltpu.VMEM((SHARD, 2 * HD), f32),
         ),
         in_specs=[any_space] * 5 + [pl.BlockSpec(memory_space=pltpu.SMEM)],
-        out_specs=(vmem_space, any_space, vmem_space, vmem_space),
+        out_specs=(vmem_space,) * 4,
         scratch_shapes=[
             pltpu.VMEM((ROWS, WIDTH), bf16),
             pltpu.VMEM((ROWS, 2048), bf16),
@@ -503,7 +511,7 @@
             pltpu.VMEM(block, bf16),
             pltpu.VMEM(block, bf16),
             pltpu.VMEM(block, bf16),
-            pltpu.VMEM((TILES, ROWS, TILE), bf16),
+            pltpu.VMEM((2, ROWS, TILE), bf16),
             pltpu.VMEM((TILES, ROWS, TILE), bf16),
             pltpu.VMEM((TILES, ROWS, TILE), bf16),
             pltpu.VMEM((2, ROWS, TILE), bf16),
@@ -514,7 +522,7 @@
             pltpu.SemaphoreType.DMA((LOCAL_SEMS,)),
         ],
         compiler_params=pltpu.CompilerParams(
-            collective_id=0, has_side_effects=True, vmem_limit_bytes=56 * 1024 * 1024
+            collective_id=0, has_side_effects=True, vmem_limit_bytes=53 * 1024 * 1024
         ),
         cost_estimate=pl.CostEstimate(flops=18_000_000_000, bytes_accessed=24_000_000, transcendentals=2_100_000),
     )(hidden_in[0], queries[0], out_grad[0], key_weight[0], value_weight[0], doc_lengths[0])

time: 163 us -> 160 us (0.982)
  Pallas kernels: 156 us -> 153 us
    pallas_call x1, Pallas kernels: 156 us -> 153 us  [body(): pl.pallas_call(kernel, out_shape=(pltpu.VMEM((ROWS, 2048), bf16), pltpu.V...]
    unnamed x6 -> x4, local copies, waits for them, and re-layouts: 6.28 us -> 5.27 us
where the time goes in v6:
time: 160 us; the launch traced here: 159 us
  Pallas kernels  153 us (96%)
  local copies, waits for them, and re-layouts  5.27 us (3%)
    pallas_call x1, Pallas kernels, body(): pl.pallas_call(kernel, out_shape=(pltpu.VMEM((ROWS, 2048), bf16), pltpu.V...  153 us
    unnamed x4, local copies, waits for them, and re-layouts  5.27 us

profile of v6, /device:TPU:1, one launch (start us, length us, event | category | flops | bytes accessed | tf_op | source)
XLA Modules:
  0.0 159.4 jit_solution(10926155148495609729)
XLA Ops:
  0.6 153.5 %shard_map.93 = (bf16[512,2048]{1,0:T(8,128)(2,1)S(1)}, bf16[512,4096]{1,0:T(8,128)(2,1)S(1)}, f32[1024,256]{1,0:T(8,128)S(1)}, f32[1024,256]{1,0:T(8,128)S(1)}) custom-call(bf16[512,8192]{1,0:T(8,128)(2,1)} %bitcast.14, bf16[512,2048]{1,0:T(8,128)(2,1)} %bitcast.15, bf16[512,2048]{1,0:T(8,128)(2,1)} %bitcast.16, bf16[1024,256]{1,0:T(8,128)(2,1)} %bitcast.17, ...), custom_call_target="tpu_custom_call" | custom-call | flops 17999998976 | bytes 24000000 | tf_op jit(solution)/shard_map/pallas_call | solution.py:483
  154.1 1.3 copy.14
  155.5 2.0 %copy.15 = bf16[1,512,4096]{2,1,0:T(8,128)(2,1)} copy(bf16[1,512,4096]{2,1,0:T(8,128)(2,1)S(1)} %bitcast.10) | data formatting | bytes 8388608
  157.5 1.0 copy.16
  158.4 1.0 copy.17

commit v7 on v6

--- a/solution.py
+++ b/solution.py
@@ -29,7 +29,9 @@
 HOP3_SEM = HOP2_SEM + 2
 RELAY_SEM = HOP3_SEM + 2
 PASS_SEM = RELAY_SEM + 3
-REMOTE_SEMS = PASS_SEM + 3
+TAIL_SEM = PASS_SEM + 3
+TAIL_PASS_SEM = TAIL_SEM + 1
+REMOTE_SEMS = TAIL_PASS_SEM + 1
 LONG_TILES = (1, 3)
 RELAY_TILES = (0, 2, 4)
 DIRECT_TILES = (5, 6, 7)
@@ -342,11 +344,29 @@
     def pp_copy(t):
         return remote(lgo.at[t], out_tile(t), PP_SEM + t, dev_prev)
 
+    first_rows, tail_rows = pl.ds(0, ROWS // 2), pl.ds(ROWS // 2, ROWS // 2)
+    tail_tile = RELAY_TILES[2]
+
+    def out_rows(t, rows):
+        return lg_ref.at[rows, pl.ds(t * TILE, TILE)]
+
     def relay_copy(i, t):
         return remote(lgo.at[t], held.at[i], RELAY_SEM + i, dev_down)
 
     def pass_copy(i, t):
         return remote(held.at[i], out_tile(t), PASS_SEM + i, dev_far, PP_SEM + t)
+
+    def first_relay():
+        return remote(lgo.at[tail_tile, first_rows], held.at[2, first_rows], RELAY_SEM + 2, dev_down)
+
+    def tail_relay():
+        return remote(lgo.at[tail_tile, tail_rows], held.at[2, tail_rows], TAIL_SEM, dev_down)
+
+    def first_pass():
+        return remote(held.at[2, first_rows], out_rows(tail_tile, first_rows), PASS_SEM + 2, dev_far, PP_SEM + tail_tile)
+
+    def tail_pass():
+        return remote(held.at[2, tail_rows], out_rows(tail_tile, tail_rows), TAIL_PASS_SEM, dev_far)
 
     def hop1_copy(i, t):
         return remote(lgo.at[t], hop1.at[i], HOP1_SEM + i, dev_up)
@@ -368,12 +388,18 @@
     def pass_on(i):
         @pl.when(z == 3)
         def _():
-            relay_copy(i, RELAY_TILES[i]).wait_recv()
-            pass_copy(i, RELAY_TILES[i]).start()
+            if i == 2:
+                first_relay().wait_recv()
+                first_pass().start()
+                tail_relay().wait_recv()
+                tail_pass().start()
+            else:
+                relay_copy(i, RELAY_TILES[i]).wait_recv()
+                pass_copy(i, RELAY_TILES[i]).start()
 
     def send_tile(t):
         is_long = (t == LONG_TILES[0]) | (t == LONG_TILES[1])
-        is_relay = (z == 0) & ((t == RELAY_TILES[0]) | (t == RELAY_TILES[1]) | (t == RELAY_TILES[2]))
+        is_relay = (z == 0) & ((t == RELAY_TILES[0]) | (t == RELAY_TILES[1]))
 
         @pl.when(is_long)
         def _():
@@ -382,6 +408,13 @@
         @pl.when(is_relay)
         def _():
             relay_copy(t // 2, t).start()
+
+        is_tail = (z == 0) & (t == tail_tile)
+
+        @pl.when(is_tail)
+        def _():
+            first_relay().start()
+            tail_relay().start()
 
         @pl.when(jnp.logical_not(is_long) & ((z != 0) | (t == DIRECT_TILES[0])))
         def _():
@@ -460,8 +493,11 @@
 
         @pl.when(z == 0)
         def _(i=i, t=t):
-            if i != 1:
+            if i == 0:
                 relay_copy(i, t).wait_send()
+            if i == 2:
+                first_relay().wait_send()
+                tail_relay().wait_send()
 
         @pl.when(z != 0)
         def _(t=t):
@@ -469,10 +505,24 @@
 
         @pl.when(z == 3)
         def _(i=i, t=t):
-            pass_copy(i, t).wait_send()
+            if i == 2:
+                first_pass().wait_send()
+                tail_pass().wait_send()
+            else:
+                pass_copy(i, t).wait_send()
+
+    @pl.when(z == 3)
+    def _():
+        first_pass().wait_recv()
+        tail_pass().wait_recv()
+
+    @pl.when(z != 3)
+    def _():
+        pp_copy(tail_tile).wait_recv()
 
     for t in range(TILES):
-        pp_copy(t).wait_recv()
+        if t != tail_tile:
+            pp_copy(t).wait_recv()
 
 
 def body(hidden_in, queries, out_grad, key_weight, value_weight, doc_lengths):

time: 160 us -> 160 us (level)
  no operation moved by 1% of the time
where the time goes in v7:
time: 160 us; the launch traced here: 159 us
  Pallas kernels  154 us (96%)
  local copies, waits for them, and re-layouts  5.27 us (3%)
    pallas_call x1, Pallas kernels, body(): pl.pallas_call(kernel, out_shape=(pltpu.VMEM((ROWS, 2048), bf16), pltpu.V...  154 us
    unnamed x4, local copies, waits for them, and re-layouts  5.27 us

profile of v7, /device:TPU:1, one launch (start us, length us, event | category | flops | bytes accessed | tf_op | source)
XLA Modules:
  0.0 159.5 jit_solution(148016592015644637)
XLA Ops:
  0.6 153.6 %shard_map.93 = (bf16[512,2048]{1,0:T(8,128)(2,1)S(1)}, bf16[512,4096]{1,0:T(8,128)(2,1)S(1)}, f32[1024,256]{1,0:T(8,128)S(1)}, f32[1024,256]{1,0:T(8,128)S(1)}) custom-call(bf16[512,8192]{1,0:T(8,128)(2,1)} %bitcast.14, bf16[512,2048]{1,0:T(8,128)(2,1)} %bitcast.15, bf16[512,2048]{1,0:T(8,128)(2,1)} %bitcast.16, bf16[1024,256]{1,0:T(8,128)(2,1)} %bitcast.17, ...), custom_call_target="tpu_custom_call" | custom-call | flops 17999998976 | bytes 24000000 | tf_op jit(solution)/shard_map/pallas_call | solution.py:533
  154.2 1.3 copy.14
  155.5 2.0 %copy.15 = bf16[1,512,4096]{2,1,0:T(8,128)(2,1)} copy(bf16[1,512,4096]{2,1,0:T(8,128)(2,1)S(1)} %bitcast.10) | data formatting | bytes 8388608
  157.5 1.0 copy.16
  158.5 1.0 copy.17
